TPU v7x, 512 devices: a whole 4x8x8 slice. The times are simulated.
512 devices in a mesh: expert: 128 (over z, y, core), tensor: 4 (over x).
Axes of the slice: x: 4, y: 8, z: 8, core: 2. Of those that a mesh axis runs over, the one named last changes fastest.
Arguments:
- hidden_rows: bfloat16 [2048, 8, 1024], P('expert', None, 'tensor'), may hold values from -16 to 16
- route_ids: int32 [2048, 8], P('expert'), may hold values from 0 to 127, all different within a row; in each aligned block of 16 rows (0 to 15, 16 to 31, ...) at most 2 rows name the same one
- route_weights: float32 [2048, 8], P('expert'), may hold values from 0.02 to 0.25
- code_fp8: bfloat16 [128, 1024, 3584], P('expert', None, 'tensor'), may hold values from -1.875 to 1.875, as said below
- scale_fp8: float32 [128, 8, 28], P('expert', None, 'tensor'), as said below
- code_int4: bfloat16 [128, 1024, 3584], P('expert', None, 'tensor'), may hold values from -7 to 7, as said below
- scale_int4: float32 [128, 8, 3584], P('expert', None, 'tensor'), as said below
Outputs:
- mixed: bfloat16 [2048, 3584], P('expert', 'tensor')
- token_error: float32 [2048], P('expert')
- expert_ratio: float32 [128], P('expert')
Inputs may be any that keep to these rules, and one draw needn't show every extreme that they name: `route_ids`: in each aligned block of 16 tokens (the tokens of one index of the expert axis), every expert is named by at most 2 routes; the 8 routes of a token name different experts; every expert is named somewhere. `code_fp8`: values of the E4M3 format: a sign times (8 + m) * 2**q / 64 with m from 0 to 7 and q from 0 to 3. `code_int4`: Integers. `scale_fp8`: Positive. `scale_int4`: Positive.
All inputs are finite; a program needn't handle non-finite values.
Results may differ from a plain program's by a relative error of at most 0.0058.
Values may be sent and summed in bfloat16 or wider, within the bound.
A program may use at most 64 MiB of HBM per device.

v0:
```python
import jax
import jax.numpy as jnp
from jax import lax
from jax.sharding import PartitionSpec as P

BLOCK = 128


def dequantize(fp8_codes, fp8_scales, int4_codes, int4_scales):
    owned, inner, outer = fp8_codes.shape
    fp8_full = (
        fp8_codes.astype(jnp.float32).reshape(owned, inner // BLOCK, BLOCK, outer // BLOCK, BLOCK)
        * fp8_scales[:, :, None, :, None]
    )
    int4_full = (
        int4_codes.astype(jnp.float32).reshape(owned, inner // BLOCK, BLOCK, outer)
        * int4_scales[:, :, None, :]
    )
    return (
        fp8_full.reshape(owned, inner, outer).astype(jnp.bfloat16),
        int4_full.reshape(owned, inner, outer).astype(jnp.bfloat16),
    )


def slot_numbers(route_ids, experts, capacity):
    flat_ids = route_ids.reshape(-1)
    onehot = (flat_ids[:, None] == jnp.arange(experts, dtype=jnp.int32)[None, :]).astype(jnp.int32)
    position = jnp.sum((jnp.cumsum(onehot, axis=0) - 1) * onehot, axis=1)
    return flat_ids * capacity + position


def per_device(hidden_rows, route_ids, route_weights, code_fp8, scale_fp8, code_int4, scale_int4):
    tok_dev, top_count, part_width = hidden_rows.shape
    exp_dev = code_fp8.shape[0]
    experts = exp_dev * lax.axis_size("expert")
    capacity = max(2, min(tok_dev, (3 * tok_dev * top_count + 2 * experts - 1) // (2 * experts)))
    slots = slot_numbers(route_ids, experts, capacity)
    weight_fp8, weight_int4 = dequantize(code_fp8, scale_fp8, code_int4, scale_int4)
    width = hidden_rows.shape[2]
    buffer = (
        jnp.zeros((experts * capacity, width), jnp.bfloat16)
        .at[slots]
        .set(hidden_rows.reshape(-1, width))
    )
    arrived = lax.all_to_all(
        buffer.reshape(experts, capacity, width), "expert", split_axis=0, concat_axis=1, tiled=True
    )
    piece = lax.all_gather(arrived, "tensor", axis=2, tiled=True)
    sum_fp8 = jnp.einsum("erf,efd->erd", piece, weight_fp8, preferred_element_type=jnp.float32)
    sum_int4 = jnp.einsum("erf,efd->erd", piece, weight_int4, preferred_element_type=jnp.float32)
    result_fp8 = sum_fp8.astype(jnp.bfloat16)
    result_int4 = sum_int4.astype(jnp.bfloat16)
    fp8_value = result_fp8.astype(jnp.float32)
    deviation = result_int4.astype(jnp.float32) - fp8_value
    ref_part = jnp.sum(fp8_value * fp8_value, axis=(1, 2))
    gate_flat = route_weights.reshape(-1)
    error_part = jnp.sum(deviation * deviation, axis=(1, 2))
    error_total, ref_total = lax.psum((error_part, ref_part), "tensor")
    back_fp8, back_int4 = (
        lax.all_to_all(result_fp8, "expert", split_axis=1, concat_axis=0, tiled=True),
        lax.all_to_all(result_int4, "expert", split_axis=1, concat_axis=0, tiled=True),
    )
    route_gap = back_int4.reshape(experts * capacity, -1)[slots].astype(
        jnp.float32
    ) - back_fp8.reshape(experts * capacity, -1)[slots].astype(jnp.float32)
    token_part = jnp.sum(
        (gate_flat * jnp.sum(route_gap * route_gap, axis=1)).reshape(tok_dev, top_count), axis=1
    )
    token_error = lax.psum(token_part, "tensor")
    route_fp8 = back_fp8.reshape(experts * capacity, -1)[slots].astype(jnp.float32)
    mixed = jnp.sum(
        (gate_flat[:, None] * route_fp8).reshape(tok_dev, top_count, -1), axis=1
    ).astype(jnp.bfloat16)
    expert_ratio = error_total / (ref_total + 1e-06)
    return (mixed, token_error, expert_ratio)


def solution(mesh):
    return jax.shard_map(
        per_device,
        mesh=mesh,
        in_specs=(
            P("expert", None, "tensor"),
            P("expert", None),
            P("expert", None),
            P("expert", None, "tensor"),
            P("expert", None, "tensor"),
            P("expert", None, "tensor"),
            P("expert", None, "tensor"),
        ),
        out_specs=(P("expert", "tensor"), P("expert"), P("expert")),
        check_vma=False,
    )
```

profile of v0, /device:TPU:1, one launch (start us, length us, event | category | flops | bytes accessed | tf_op | source)
XLA Modules:
  0.0 132.3 jit_solution(5551394529637826418)
XLA Ops:
  0.6 0.0 copy-start
  0.6 0.8 copy.33
  1.4 0.7 broadcast_multiply_fusion
  2.1 0.1 eq.15
  2.2 0.1 fusion.19
  2.3 0.2 reduce_window_sum.11
  2.5 0.2 select_reduce_fusion
  2.7 0.1 copy.32
  2.7 0.1 mul.78
  2.8 1.1 scatter_custom_fusion
  3.9 0.7 reshape.121
  4.6 18.4 %all-to-all-start = ((bf16[128,2,256]{2,1,0:T(2,128)(2,1)}), bf16[128,2,256]{2,1,0:T(2,128)(2,1)S(1)}, u32[]{:S(2)}, u32[]{:S(2)}) async-start(bf16[128,2,256]{2,1,0:T(2,128)(2,1)} %reshape.121), calls=%async_computation | async-start | bytes 262144 | tf_op jit(solution)/shard_map/all_to_all | solution.py:45
  23.1 0.7 copy.50
  23.7 2.1 %mul.81 = f32[8,128,7,128]{1,0,3,2:T(8,128)} broadcast(f32[8,7]{0,1:T(8,128)S(1)} %bitcast.76), dimensions={0,2} | broadcast | bytes 3670240 | tf_op jit(solution)/shard_map/mul | solution.py:12
  25.9 4.7 %mul.82 = f32[1,1024,896]{1,2,0:T(8,128)} reshape(f32[8,128,7,128]{1,0,3,2:T(8,128)} %mul.81) | data formatting | bytes 7340032 | tf_op jit(solution)/shard_map/mul | solution.py:12
  30.6 2.9 %copy.34 = bf16[1,1024,896]{1,2,0:T(8,128)(2,1)S(1)} copy(bf16[1,1024,896]{2,1,0:T(8,128)(2,1)} %param.10) | data formatting | bytes 3670016 | tf_op args[3]
  33.5 0.0 copy-start.2
  33.5 0.2 mul.86
  33.8 1.2 copy-done.2
  35.0 1.6 %fusion.4 = bf16[1024,896]{1,0:T(8,128)(2,1)} fusion(bf16[1,1024,896]{2,1,0:T(8,128)(2,1)S(1)} %copy-done.2, f32[1,1024,896]{2,1,0:T(8,128)S(1)} %bitcast.66), kind=kLoop, calls=%fused_computation.8 | loop fusion | flops 2752512 | bytes 7340032 | tf_op jit(solution)/shard_map/reshape.11
  36.6 0.1 all_to_all.9
  36.7 11.8 %all_gather.3 = bf16[1,256,1024]{2,1,0:T(8,128)(2,1)S(1)} all-gather(bf16[1,256,256]{2,1,0:T(8,128)(2,1)S(1)} %all_to_all.9), channel_id=1, replica_groups=mesh['expert'=128,'tensor'=4] {'tensor'}, dimensions={2}, use_global_device_ids=true | all-gather | bytes 655360 | tf_op jit(solution)/shard_map/all_gather | solution.py:48
  48.5 2.2 %convolution_convert_fusion = bf16[256,896]{1,0:T(8,128)(2,1)S(1)} fusion(bf16[1024,896]{1,0:T(8,128)(2,1)} %fusion.4, bf16[1,256,1024]{2,1,0:T(8,128)(2,1)S(1)} %all_gather.3), kind=kOutput, calls=%fused_computation.9 | convolution fusion | flops 469991424 | bytes 2818048 | tf_op jit(solution)/shard_map/erf,efd->erd/dot_general | solution.py:50
  50.8 1.6 %fusion.10 = (f32[]{:T(128)}, f32[]{:T(128)}, bf16[256,896]{1,0:T(8,128)(2,1)S(1)}) fusion(bf16[256,896]{1,0:T(8,128)(2,1)S(1)} %convolution_convert_fusion, f32[1,1024,896]{1,2,0:T(8,128)S(1)} %copy-done.1, bf16[1,1024,896]{1,2,0:T(8,128)(2,1)S(1)} %copy.34, bf16[1,256,1024]{2,1,0:T(8,128)(2,1)S(1)} %all_gather.3), kind=kOutput, calls=%fused_computation.15 | convolution fusion | flops 474349568 | bytes 6946824 | tf_op jit(solution)/shard_map/erf,efd->erd/dot_general | solution.py:49
  52.3 0.7 copy.52
  53.1 0.5 broadcast.60
  53.6 3.4 %reduce.4 = bf16[256,896]{1,0:T(8,128)(2,1)S(1)} reduce(bf16[256,1,896]{2,1,0:T(2,128)(2,1)S(1)} %bitcast.69, bf16[]{:T(256)} %broadcast.60), dimensions={1}, to_apply=%bitcast.64.reduce_sub_computation | reduce | bytes 917506
  57.0 0.9 reshape.154
  57.9 15.2 %all-to-all-start.1 = ((bf16[128,2,896]{2,1,0:T(2,128)(2,1)}), bf16[128,2,896]{2,1,0:T(2,128)(2,1)S(1)}, u32[]{:S(2)}, u32[]{:S(2)}) async-start(bf16[128,2,896]{2,1,0:T(2,128)(2,1)} %reshape.154), calls=%async_computation.1 | async-start | bytes 917504 | tf_op jit(solution)/shard_map/all_to_all | solution.py:60
  73.1 0.7 copy.51
  73.8 0.0 copy-start.4
  73.8 3.4 %reduce.5 = bf16[256,896]{1,0:T(8,128)(2,1)S(1)} reduce(bf16[256,1,896]{2,1,0:T(2,128)(2,1)S(1)} %bitcast.70, bf16[]{:T(256)} %broadcast.60), dimensions={1}, to_apply=%bitcast.63.reduce_sub_computation | reduce | bytes 917506
  77.2 1.0 reshape.156
  78.2 14.2 %all-to-all-done.1 = bf16[128,2,896]{2,1,0:T(2,128)(2,1)S(1)} async-done(((bf16[128,2,896]{2,1,0:T(2,128)(2,1)}), bf16[128,2,896]{2,1,0:T(2,128)(2,1)S(1)}, u32[]{:S(2)}, u32[]{:S(2)}) %all-to-all-start.1) | async-done | bytes 458784 | tf_op jit(solution)/shard_map/all_to_all | solution.py:60
  92.3 5.3 %all-to-all-start.2 = ((bf16[128,2,896]{2,1,0:T(2,128)(2,1)}), bf16[128,2,896]{2,1,0:T(2,128)(2,1)S(1)}, u32[]{:S(2)}, u32[]{:S(2)}) async-start(bf16[128,2,896]{2,1,0:T(2,128)(2,1)} %reshape.156), calls=%async_computation.2 | async-start | bytes 917504 | tf_op jit(solution)/shard_map/all_to_all | solution.py:61
  97.7 0.1 copy.31
  97.8 0.4 reshape.155
  98.1 0.1 copy.49
  98.2 18.7 %all-to-all-done.2 = bf16[128,2,896]{2,1,0:T(2,128)(2,1)S(1)} async-done(((bf16[128,2,896]{2,1,0:T(2,128)(2,1)}), bf16[128,2,896]{2,1,0:T(2,128)(2,1)S(1)}, u32[]{:S(2)}, u32[]{:S(2)}) %all-to-all-start.2) | async-done | bytes 458784 | tf_op jit(solution)/shard_map/all_to_all | solution.py:61
  116.9 0.4 reshape.157
  117.3 0.1 copy.48
  117.4 0.9 gather_fusion
  118.2 0.9 gather_fusion.1
  119.1 0.2 fusion.16
  119.3 0.1 reduce_sum.66
  119.4 0.8 fusion.14
  120.2 0.1 multiply_reduce_fusion
  120.3 9.5 %all-reduce = (f32[16]{0:T(128)}, f32[1]{0:T(128)}, f32[1]{0:T(128)}) all-reduce(f32[16]{0:T(128)S(1)} %multiply_reduce_fusion, f32[1]{0:T(128)} %bitcast.13, f32[1]{0:T(128)} %bitcast.14), channel_id=1, replica_groups=mesh['expert'=128,'tensor'=4] {'tensor'}, use_global_device_ids=true, to_apply=%region_6.7 | all-reduce | flops 18 | bytes 144 | tf_op jit(solution)/shard_map/psum | solution.py:69
  (9 shorter events, 0.0 us)
Async XLA Ops:
  0.6 2.2 %copy-start = (bf16[16,8,256]{2,1,0:T(8,128)(2,1)S(1)}, bf16[16,8,256]{2,1,0:T(8,128)(2,1)}, u32[]{:S(2)}) copy-start(bf16[16,8,256]{2,1,0:T(8,128)(2,1)} %param.7) | copy-start | bytes 196612
  4.6 32.0 %all-to-all-start = ((bf16[128,2,256]{2,1,0:T(2,128)(2,1)}), bf16[128,2,256]{2,1,0:T(2,128)(2,1)S(1)}, u32[]{:S(2)}, u32[]{:S(2)}) async-start(bf16[128,2,256]{2,1,0:T(2,128)(2,1)} %reshape.121), calls=%async_computation | async-start | bytes 262144 | tf_op jit(solution)/shard_map/all_to_all | solution.py:45
  30.6 2.9 %copy-start.3 = (f32[1,8,896]{2,1,0:T(8,128)S(1)}, f32[1,8,896]{2,1,0:T(8,128)}, u32[]{:S(2)}) copy-start(f32[1,8,896]{2,1,0:T(8,128)} %param.13) | copy-start | bytes 86020
  33.5 1.5 %copy-start.2 = (bf16[1,1024,896]{2,1,0:T(8,128)(2,1)S(1)}, bf16[1,1024,896]{2,1,0:T(8,128)(2,1)}, u32[]{:S(2)}) copy-start(bf16[1,1024,896]{2,1,0:T(8,128)(2,1)} %param.12) | copy-start | bytes 5505028
  36.7 14.1 %copy-start.1 = (f32[1,1024,896]{1,2,0:T(8,128)S(1)}, f32[1,1024,896]{1,2,0:T(8,128)}, u32[]{:S(2)}) copy-start(f32[1,1024,896]{1,2,0:T(8,128)} %mul.82) | copy-start | bytes 11010052
  57.9 34.4 %all-to-all-start.1 = ((bf16[128,2,896]{2,1,0:T(2,128)(2,1)}), bf16[128,2,896]{2,1,0:T(2,128)(2,1)S(1)}, u32[]{:S(2)}, u32[]{:S(2)}) async-start(bf16[128,2,896]{2,1,0:T(2,128)(2,1)} %reshape.154), calls=%async_computation.1 | async-start | bytes 917504 | tf_op jit(solution)/shard_map/all_to_all | solution.py:60
  73.8 23.9 %copy-start.4 = (f32[16,8]{0,1:T(8,128)S(1)}, f32[16,8]{0,1:T(8,128)}, u32[]{:S(2)}) copy-start(f32[16,8]{0,1:T(8,128)} %param.9) | copy-start | bytes 1540
  92.3 24.6 %all-to-all-start.2 = ((bf16[128,2,896]{2,1,0:T(2,128)(2,1)}), bf16[128,2,896]{2,1,0:T(2,128)(2,1)S(1)}, u32[]{:S(2)}, u32[]{:S(2)}) async-start(bf16[128,2,896]{2,1,0:T(2,128)(2,1)} %reshape.156), calls=%async_computation.2 | async-start | bytes 917504 | tf_op jit(solution)/shard_map/all_to_all | solution.py:61
where the time goes:
time: 134 us; the launch traced here: 132 us
  starting transfers between devices  38.9 us (29%)
  waiting for transfers between devices  32.9 us (25%)
  local copies, waits for them, and re-layouts  21.4 us (16%)
  blocking collectives  21.4 us (16%)
  other arithmetic  10.6 us (8%)
  matrix products  3.78 us (3%)
  between operations  3.32 us (2%)
    all_to_all x1, waiting for transfers between devices, per_device(): lax.all_to_all(result_int4, 'expert', split_axis=1, concat_axis=0, tiled=...  18.7 us
    all_to_all x1, starting transfers between devices, per_device(): lax.all_to_all(buffer.reshape(experts, capacity, width), 'expert', split_...  18.4 us
    all_to_all x1, starting transfers between devices, per_device(): lax.all_to_all(result_fp8, 'expert', split_axis=1, concat_axis=0, tiled=T...  15.2 us
    all_to_all x1, waiting for transfers between devices, per_device(): lax.all_to_all(result_fp8, 'expert', split_axis=1, concat_axis=0, tiled=T...  14.2 us
    all_gather x1, blocking collectives, per_device(): piece = lax.all_gather(arrived, 'tensor', axis=2, tiled=True)  11.8 us
    psum x1, blocking collectives, per_device(): token_error = lax.psum(token_part, 'tensor')  9.52 us
    unnamed x20, local copies, waits for them, and re-layouts  8.28 us
    mul x3, local copies, waits for them, and re-layouts, dequantize(): fp8_codes.astype(jnp.float32)  7.56 us
  transfers between devices with their start and end apart: 3, of which 2 were waited for; matrix products, arithmetic and copies ran while one was open for 14% of the time, Pallas kernels for 0%

commit v1 on v0

v1 whole, which is shorter than its diff:
```python
import functools

import jax
import jax.numpy as jnp
from jax import lax
from jax.experimental import pallas as pl
from jax.experimental.pallas import tpu as pltpu
from jax.sharding import PartitionSpec as P

BLOCK = 128
SLOTS = 2
COLUMN = 8
MESH = pl.DeviceIdType.MESH
f32, bf16 = jnp.float32, jnp.bfloat16


def iota(shape, dim):
    return lax.broadcasted_iota(jnp.int32, shape, dim)


def dot(a, b):
    return jnp.dot(a, b, preferred_element_type=f32)


def split3(value):
    high = value.astype(bf16).astype(f32)
    rest = value - high
    middle = rest.astype(bf16).astype(f32)
    return high, middle, rest - middle


def chunks_of(width):
    full = 2 * BLOCK
    starts = list(range(0, width, full))
    return [(s, min(full, width - s)) for s in starts]


def kernel(
    sizes,
    ids_ref, gate_ref, hidden_ref, scale8_ref, scale4_ref, code8_ref, code4_ref,
    mixed_ref, token_ref, ratio_ref,
    w8, w4, send1, gates1, recv1, grecv, send2, x_all, out8, back1, part, back2, sums, sums_all,
    code_sem, s1, r1, sg, rg, s2, r2, sx, rx, se, re, sb, rb, sc, rc,
):
    zs, rs, xs, tok, top = sizes
    routes = tok * top
    rows = zs * rs * SLOTS
    z_rows, r_rows = rs * SLOTS, zs * SLOTS
    width = hidden_ref.shape[1]
    inner, feats = w8.shape
    chunks = chunks_of(feats)

    me, tn = lax.axis_index("expert"), lax.axis_index("tensor")
    z, r = me // rs, lax.rem(me, rs)

    def in_column(d):
        return lax.rem(z + d, zs)

    def in_row(d):
        return lax.rem(r + d, rs)

    def in_gather(d):
        return lax.rem(tn + d, xs)

    part_rows = inner // 2
    code_copies = []
    for n, (src, dst) in enumerate(((code8_ref, w8), (code4_ref, w4))):
        for h in range(2):
            piece = pl.ds(h * part_rows, part_rows)
            copy = pltpu.make_async_copy(src.at[0, piece, :], dst.at[piece, :], code_sem.at[n, h])
            copy.start()
            code_copies.append(copy)

    barrier = pltpu.get_barrier_semaphore()

    @pl.loop(1, zs)
    def _(d):
        pl.semaphore_signal(
            barrier, inc=1, device_id={"expert": in_column(d) * rs + r}, device_id_type=MESH
        )

    @pl.loop(1, rs)
    def _(d):
        pl.semaphore_signal(
            barrier, inc=1, device_id={"expert": z * rs + in_row(d)}, device_id_type=MESH
        )

    @pl.loop(1, xs)
    def _(d):
        pl.semaphore_signal(barrier, inc=1, device_id={"tensor": in_gather(d)}, device_id_type=MESH)

    ids = jnp.broadcast_to(ids_ref[...], (routes, routes))
    earlier = (ids == ids.T) & (iota((routes, routes), 0) < iota((routes, routes), 1))
    position = jnp.sum(earlier.astype(jnp.int32), axis=0, keepdims=True)
    target = ids_ref[...] * SLOTS + position
    chosen = iota((rows, routes), 0) == target
    select = chosen.astype(f32).astype(bf16)
    gate = gate_ref[...]
    gate_high = gate.astype(bf16).astype(f32)
    gate_low = gate - gate_high
    lanes = gates1.shape[1]
    token_of = iota((routes, lanes), 0) // top
    place = iota((routes, lanes), 1)
    spread_high = (place == token_of).astype(f32).astype(bf16)
    spread_low = (place == token_of + tok).astype(f32).astype(bf16)
    send1[...] = dot(select, hidden_ref[...]).astype(bf16)
    gates1[...] = (
        dot(jnp.where(chosen, gate_high, 0.0).astype(bf16), spread_high)
        + dot(jnp.where(chosen, gate_low, 0.0).astype(bf16), spread_low)
    ).astype(bf16)

    pl.semaphore_wait(barrier, zs + rs + xs - 3)

    def column_copy(src, dst, there, send, recv):
        return pltpu.make_async_remote_copy(
            src_ref=src,
            dst_ref=dst,
            send_sem=send,
            recv_sem=recv,
            device_id={"expert": there * rs + r},
            device_id_type=MESH,
        )

    def row_copy(src, dst, there, send, recv):
        return pltpu.make_async_remote_copy(
            src_ref=src,
            dst_ref=dst,
            send_sem=send,
            recv_sem=recv,
            device_id={"expert": z * rs + there},
            device_id_type=MESH,
        )

    def gather_copy(src, dst, there, send, recv):
        return pltpu.make_async_remote_copy(
            src_ref=src,
            dst_ref=dst,
            send_sem=send,
            recv_sem=recv,
            device_id={"tensor": there},
            device_id_type=MESH,
        )

    def z_block(n):
        return pl.ds(pl.multiple_of(n * z_rows, z_rows), z_rows)

    def r_block(n):
        return pl.ds(pl.multiple_of(n * r_rows, r_rows), r_rows)

    def t_block(n):
        return pl.ds(pl.multiple_of(n * tok, tok), tok)

    @pl.loop(1, zs)
    def _(d):
        there = in_column(d)
        column_copy(send1.at[z_block(there)], recv1.at[z_block(z)], there, s1, r1).start()

    @pl.loop(1, zs)
    def _(d):
        there = in_column(d)
        column_copy(gates1.at[z_block(there)], grecv.at[z_block(z)], there, sg, rg).start()

    recv1[z_block(z), :] = send1[z_block(z), :]
    grecv[z_block(z), :] = gates1[z_block(z), :]

    def scale_weights(first, last):
        @pl.loop(first, last)
        def _(g):
            group = pl.ds(pl.multiple_of(g * BLOCK, BLOCK), BLOCK)
            for b in range(feats // BLOCK):
                cols = pl.ds(b * BLOCK, BLOCK)
                w8[group, cols] = (w8[group, cols].astype(f32) * scale8_ref[0, g, b]).astype(bf16)
            w4[group, :] = (w4[group, :].astype(f32) * scale4_ref[0, pl.ds(g, 1), :]).astype(bf16)

    groups = inner // BLOCK
    for copy in code_copies:
        copy.wait()
    scale_weights(0, groups // 4)

    at, of = iota((rows, rows), 0), iota((rows, rows), 1)
    reorder = of == (at % r_rows) // SLOTS * z_rows + at // r_rows * SLOTS + at % SLOTS
    reorder = reorder.astype(f32).astype(bf16)

    all_but_one = pl.ds(0, rows - z_rows)
    wait = column_copy(send1.at[all_but_one], recv1.at[all_but_one], z, s1, r1)
    wait.wait_recv()
    send2[...] = dot(reorder, recv1[...]).astype(bf16)

    mine = pl.ds(pl.multiple_of(tn * width, width), width)

    @pl.loop(1, rs)
    def _(d):
        there = in_row(d)
        row_copy(send2.at[r_block(there)], x_all.at[r_block(r), mine], there, s2, r2).start()

    x_all[r_block(r), mine] = send2[r_block(r), :]

    wait_g = column_copy(gates1.at[all_but_one], grecv.at[all_but_one], z, sg, rg)
    wait_g.wait_recv()
    tokens = zs * tok
    gates = dot(reorder, grecv[...]).astype(bf16)
    lane, wide = iota((lanes, 2 * tokens), 0), iota((lanes, 2 * tokens), 1)
    widen = (lane == wide % tok + jnp.where(wide < tokens, 0, tok)).astype(f32).astype(bf16)
    wide_gates = dot(gates, widen)
    row_z = iota((rows, 2 * tokens), 0) % r_rows // SLOTS
    lane_z = iota((rows, 2 * tokens), 1) % tokens // tok
    combine = jnp.where(row_z == lane_z, wide_gates, 0.0).T.astype(bf16)

    scale_weights(groups // 4, groups // 2)

    all_but_r = pl.ds(0, rows - r_rows)
    wait_2 = row_copy(send2.at[all_but_r], x_all.at[all_but_r, mine], r, s2, r2)
    wait_2.wait_recv()

    @pl.loop(1, xs)
    def _(d):
        gather_copy(x_all.at[:, mine], x_all.at[:, mine], in_gather(d), sx, rx).start()

    scale_weights(groups // 2, groups)
    others = pl.ds(0, (xs - 1) * width)
    wait_x = gather_copy(x_all.at[:, others], x_all.at[:, others], tn, sx, rx)
    wait_x.wait_recv()

    def send_back(c):
        @pl.loop(1, rs)
        def _(d):
            there = in_row(d)
            row_copy(
                out8.at[c, r_block(there)], back1.at[c, r_block(r)], there, sb.at[c], rb.at[c]
            ).start()

        back1[c, r_block(r), :] = out8[c, r_block(r), :]

    last = len(chunks) - 1
    for c, (start, size) in enumerate(chunks):
        out8[c, :, :size] = dot(x_all[...], w8[:, start : start + size]).astype(bf16)
        if c < last:
            send_back(c)
    gap_sum = jnp.zeros((rows, BLOCK), f32)
    ref_sum = jnp.zeros((rows, BLOCK), f32)
    for c, (start, size) in enumerate(chunks):
        result4 = dot(x_all[...], w4[:, start : start + size]).astype(bf16).astype(f32)
        result8 = out8[c, :, :size].astype(f32)
        gap = result4 - result8
        for b in range(size // BLOCK):
            cols = slice(b * BLOCK, (b + 1) * BLOCK)
            gap_sum += gap[:, cols] * gap[:, cols]
            ref_sum += result8[:, cols] * result8[:, cols]

    gap_row = jnp.sum(gap_sum.T, axis=0, keepdims=True)
    ref_row = jnp.sum(ref_sum.T, axis=0, keepdims=True)
    which = iota((8, rows), 0)
    sums[...] = jnp.where(which == 0, gap_row, jnp.where(which == 1, ref_row, 0.0))
    sums_all[tn] = sums[...]

    @pl.loop(1, xs)
    def _(d):
        gather_copy(sums, sums_all.at[tn], in_gather(d), se, re).start()

    def combine_and_send(c):
        wait_b = row_copy(
            out8.at[c, all_but_r], back1.at[c, all_but_r], r, sb.at[c], rb.at[c]
        )
        wait_b.wait_recv()
        both = dot(combine, back1[c])
        total = both[:tokens] + both[tokens:]
        if c == last:
            size = chunks[c][1]
            error = jnp.sum(total[:, size:], axis=1, keepdims=True)
            high, middle, low = split3(error)
            lane = iota((tokens, BLOCK), 1)
            parts = jnp.where(
                lane == 0, high, jnp.where(lane == 1, middle, jnp.where(lane == 2, low, 0.0))
            )
            part[c, :, :size] = total[:, :size].astype(bf16)
            part[c, :, size:] = parts.astype(bf16)
        else:
            part[c] = total.astype(bf16)

        @pl.loop(1, zs)
        def _(d):
            there = in_column(d)
            column_copy(
                part.at[c, t_block(there)], back2.at[c, t_block(z)], there, sc.at[c], rc.at[c]
            ).start()

        back2[c, t_block(z), :] = part[c, t_block(z), :]

    if last > 0:
        combine_and_send(0)

    sums_but = pl.ds(0, xs - 1)
    wait_e = pltpu.make_async_remote_copy(
        src_ref=sums_all.at[sums_but],
        dst_ref=sums_all.at[sums_but],
        send_sem=se,
        recv_sem=re,
        device_id={"tensor": tn},
        device_id_type=MESH,
    )
    wait_e.wait_recv()
    total = sums_all[0]
    for n in range(1, xs):
        total = total + sums_all[n]
    gap_total, ref_total = total[0:1], total[1:2]
    ratio_ref[...] = jnp.sum(gap_total, axis=1, keepdims=True) / (
        jnp.sum(ref_total, axis=1, keepdims=True) + 1e-06
    )
    high, middle, low = split3(gap_total)
    which = iota((BLOCK, rows), 0)
    stacked = jnp.where(
        which == 0, high, jnp.where(which == 1, middle, jnp.where(which == 2, low, 0.0))
    )
    size = chunks[last][1]
    out8[last, :, size:] = stacked.T.astype(bf16)
    send_back(last)

    for c in range(1, last + 1):
        combine_and_send(c)

    all_but_t = pl.ds(0, tokens - tok)
    for c, (start, size) in enumerate(chunks):
        wait_c = column_copy(part.at[c, all_but_t], back2.at[c, all_but_t], z, sc.at[c], rc.at[c])
        wait_c.wait_recv()
        total = back2[c, :tok].astype(f32)
        for n in range(1, zs):
            total = total + back2[c, n * tok : (n + 1) * tok].astype(f32)
        mixed_ref[:, start : start + size] = total[:, :size].astype(bf16)
        if c == last:
            error = jnp.sum(total[:, size:], axis=1, keepdims=True)
            diagonal = iota((tok, tok), 0) == iota((tok, tok), 1)
            token_ref[...] = jnp.sum(jnp.where(diagonal, error, 0.0), axis=0, keepdims=True)

    wait.wait_send()
    wait_g.wait_send()
    wait_2.wait_send()
    wait_x.wait_send()
    wait_e.wait_send()
    for c in range(len(chunks)):
        row_copy(
            out8.at[c, all_but_r], back1.at[c, all_but_r], r, sb.at[c], rb.at[c]
        ).wait_send()
        column_copy(
            part.at[c, all_but_t], back2.at[c, all_but_t], z, sc.at[c], rc.at[c]
        ).wait_send()


def per_device(sizes, hidden, ids, gates, code8, scale8, code4, scale4):
    zs, rs, xs, tok, top = sizes
    routes, width = tok * top, hidden.shape[2]
    rows = zs * rs * SLOTS
    inner, feats = code8.shape[1:]
    chunks = chunks_of(feats)
    count, tokens = len(chunks), zs * tok
    wide = max(chunks[-1][1] + BLOCK, chunks[0][1])
    vmem, smem = pl.BlockSpec(memory_space=pltpu.VMEM), pl.BlockSpec(memory_space=pltpu.SMEM)
    dma = pltpu.SemaphoreType.DMA
    mixed, token, ratio = pl.pallas_call(
        functools.partial(kernel, sizes),
        out_shape=(
            jax.ShapeDtypeStruct((tok, feats), bf16),
            jax.ShapeDtypeStruct((1, tok), f32),
            jax.ShapeDtypeStruct((1, 1), f32),
        ),
        in_specs=[vmem, vmem, vmem, smem, vmem]
        + [pl.BlockSpec(memory_space=pl.ANY)] * 2,
        out_specs=(vmem, vmem, vmem),
        scratch_shapes=[
            pltpu.VMEM((inner, feats), bf16),
            pltpu.VMEM((inner, feats), bf16),
            pltpu.VMEM((rows, width), bf16),
            pltpu.VMEM((rows, BLOCK), bf16),
            pltpu.VMEM((rows, width), bf16),
            pltpu.VMEM((rows, BLOCK), bf16),
            pltpu.VMEM((rows, width), bf16),
            pltpu.VMEM((rows, xs * width), bf16),
            pltpu.VMEM((count, rows, wide), bf16),
            pltpu.VMEM((count, rows, wide), bf16),
            pltpu.VMEM((count, tokens, wide), bf16),
            pltpu.VMEM((count, tokens, wide), bf16),
            pltpu.VMEM((8, rows), f32),
            pltpu.VMEM((xs, 8, rows), f32),
            dma((2, 2)),
        ]
        + [dma] * 10
        + [dma((count,))] * 4,
        compiler_params=pltpu.CompilerParams(
            collective_id=0, has_side_effects=True, vmem_limit_bytes=32 * 1024 * 1024
        ),
    )(
        ids.reshape(1, routes),
        gates.reshape(1, routes),
        hidden.reshape(routes, width),
        scale8,
        scale4,
        code8,
        code4,
    )
    return mixed, token.reshape(tok), ratio.reshape(1)


def solution(mesh):
    experts, xs = mesh.shape["expert"], mesh.shape["tensor"]
    zs = COLUMN
    rs = experts // zs

    def run(hidden, *rest):
        tok, top = hidden.shape[0] // experts, hidden.shape[1]
        mapped = jax.shard_map(
            functools.partial(per_device, (zs, rs, xs, tok, top)),
            mesh=mesh,
            in_specs=(
                P("expert", None, "tensor"),
                P("expert", None),
                P("expert", None),
                P("expert", None, "tensor"),
                P("expert", None, "tensor"),
                P("expert", None, "tensor"),
                P("expert", None, "tensor"),
            ),
            out_specs=(P("expert", "tensor"), P("expert"), P("expert")),
            check_vma=False,
        )
        return mapped(hidden, *rest)

    return run
```

time: 134 us -> 68.6 us (0.51)
  Pallas kernels: 0 us -> 57.6 us
  starting transfers between devices: 38.9 us -> 0 us
  waiting for transfers between devices: 32.9 us -> 0 us
  blocking collectives: 21.4 us -> 0 us
  local copies, waits for them, and re-layouts: 21.4 us -> 8.15 us
  other arithmetic: 10.6 us -> 0 us
  matrix products: 3.78 us -> 0 us
    pallas_call x0 -> x1, Pallas kernels: none -> 57.6 us  [per_device(): pl.pallas_call(functools.partial(kernel, sizes), out_shape=(jax.ShapeDtyp...]
    all_to_all x3 -> x0, starting transfers between devices: 38.9 us -> none  [the longest x1 18.4 us: per_device(): lax.all_to_all(buffer.reshape(experts, capacity, width), 'expert', split_...]
    all_to_all x3 -> x0, waiting for transfers between devices: 32.9 us -> none  [the longest x1 18.7 us: per_device(): lax.all_to_all(result_int4, 'expert', split_axis=1, concat_axis=0, tiled=...]
    all_gather x1 -> x0, blocking collectives: 11.8 us -> none  [per_device(): piece = lax.all_gather(arrived, 'tensor', axis=2, tiled=True)]
    psum x1 -> x0, blocking collectives: 9.52 us -> none  [per_device(): token_error = lax.psum(token_part, 'tensor')]
    mul x6 -> x0, local copies, waits for them, and re-layouts: 7.97 us -> none  [the longest x3 7.56 us: dequantize(): fp8_codes.astype(jnp.float32)]
    unnamed x2 -> x0, other arithmetic: 6.82 us -> none
    dot_general x2 -> x0, matrix products: 3.78 us -> none  [the longest x1 2.22 us: per_device(): jnp.einsum('erf,efd->erd', piece, weight_int4, preferred_element_type=jnp...]
  transfers between devices with their start and end apart: 3 -> 0, of which waited for: 2 -> 0; matrix products, arithmetic and copies ran while one was open for 14% -> 0% of each run, Pallas kernels for 0% -> 0%
where the time goes in v1:
time: 68.6 us; the launch traced here: 68.2 us
  Pallas kernels  57.6 us (84%)
  local copies, waits for them, and re-layouts  8.15 us (12%)
  between operations  2.4 us (3%)
    pallas_call x1, Pallas kernels, per_device(): pl.pallas_call(functools.partial(kernel, sizes), out_shape=(jax.ShapeDtyp...  57.6 us
    unnamed x13, local copies, waits for them, and re-layouts  7.98 us

profile of v1, /device:TPU:1, one launch (start us, length us, event | category | flops | bytes accessed | tf_op | source)
XLA Modules:
  0.0 68.2 jit_solution(15316735193638232749)
XLA Ops:
  0.6 0.8 %copy.15.scale8_ref = f32[1,8,7]{2,1,0:T(8,128)S(1)} copy(f32[1,8,7]{1,0,2:T(1,128)} %param.11) | data formatting | bytes 448 | tf_op args[4]
  1.4 0.8 %copy.13 = s32[16,8]{1,0:T(8,128)S(1)} copy(s32[16,8]{0,1:T(8,128)} %param.8) | data formatting | bytes 1024 | tf_op args[1]
  2.1 0.1 reshape.21.ids_ref
  2.2 0.8 %copy.14 = f32[16,8]{1,0:T(8,128)S(1)} copy(f32[16,8]{0,1:T(8,128)} %param.9) | data formatting | bytes 1024 | tf_op args[2]
  3.0 0.1 reshape.22.gate_ref
  3.1 0.0 copy-start
  3.1 1.5 %copy-done = bf16[1,1024,896]{2,1,0:T(8,128)(2,1)S(1)} copy-done((bf16[1,1024,896]{2,1,0:T(8,128)(2,1)S(1)}, bf16[1,1024,896]{2,1,0:T(8,128)(2,1)}, u32[]{:S(2)}) %copy-start) | copy-done | bytes 1835032
  4.6 0.0 copy-start.1
  4.6 1.5 %copy-done.1 = bf16[1,1024,896]{2,1,0:T(8,128)(2,1)S(1)} copy-done((bf16[1,1024,896]{2,1,0:T(8,128)(2,1)S(1)}, bf16[1,1024,896]{2,1,0:T(8,128)(2,1)}, u32[]{:S(2)}) %copy-start.1) | copy-done | bytes 1835032
  6.1 0.0 copy-start.2
  6.1 0.8 %copy-done.2 = bf16[16,8,256]{2,1,0:T(8,128)(2,1)S(1)} copy-done((bf16[16,8,256]{2,1,0:T(8,128)(2,1)S(1)}, bf16[16,8,256]{2,1,0:T(8,128)(2,1)}, u32[]{:S(2)}) %copy-start.2) | copy-done | bytes 65560
  6.9 0.0 copy-start.3
  6.9 0.7 %copy-done.3 = f32[1,8,896]{2,1,0:T(8,128)S(1)} copy-done((f32[1,8,896]{2,1,0:T(8,128)S(1)}, f32[1,8,896]{2,1,0:T(8,128)}, u32[]{:S(2)}) %copy-start.3) | copy-done | bytes 28696
  7.7 57.6 %shard_map.94 = (bf16[16,896]{1,0:T(8,128)(2,1)S(1)}, f32[1,16]{1,0:T(1,128)S(1)}, f32[1,1]{1,0:T(1,128)}) custom-call(s32[1,128]{1,0:T(1,128)S(1)} %reshape.21.ids_ref, f32[1,128]{1,0:T(1,128)S(1)} %reshape.22.gate_ref, bf16[128,256]{1,0:T(8,128)(2,1)S(1)} %bitcast.3, f32[1,8,7]{2,1,0:T(8,128)S(1)} %copy.15.scale8_ref, f32[1,8,896]{2,1,0:T(8,128)S(1)} %copy-done.3, ...), custom_call_target="tpu_custom_call" | custom-call | tf_op jit(solution)/shard_map/pallas_call | solution.py:358
  65.3 0.6 copy.19
  65.9 0.5 copy.20
Async XLA Ops:
  3.1 1.5 %copy-start = (bf16[1,1024,896]{2,1,0:T(8,128)(2,1)S(1)}, bf16[1,1024,896]{2,1,0:T(8,128)(2,1)}, u32[]{:S(2)}) copy-start(bf16[1,1024,896]{2,1,0:T(8,128)(2,1)} %code8_ref.1) | copy-start | bytes 5505028
  4.6 1.5 %copy-start.1 = (bf16[1,1024,896]{2,1,0:T(8,128)(2,1)S(1)}, bf16[1,1024,896]{2,1,0:T(8,128)(2,1)}, u32[]{:S(2)}) copy-start(bf16[1,1024,896]{2,1,0:T(8,128)(2,1)} %code4_ref.1) | copy-start | bytes 5505028
  6.1 0.8 %copy-start.2 = (bf16[16,8,256]{2,1,0:T(8,128)(2,1)S(1)}, bf16[16,8,256]{2,1,0:T(8,128)(2,1)}, u32[]{:S(2)}) copy-start(bf16[16,8,256]{2,1,0:T(8,128)(2,1)} %param.7) | copy-start | bytes 196612
  6.9 0.7 %copy-start.3 = (f32[1,8,896]{2,1,0:T(8,128)S(1)}, f32[1,8,896]{2,1,0:T(8,128)}, u32[]{:S(2)}) copy-start(f32[1,8,896]{2,1,0:T(8,128)} %scale4_ref.1) | copy-start | bytes 86020

commit v2 on v1

--- a/solution.py
+++ b/solution.py
@@ -37,10 +37,10 @@
 
 def kernel(
     sizes,
-    ids_ref, gate_ref, hidden_ref, scale8_ref, scale4_ref, code8_ref, code4_ref,
+    ids_hbm, gate_hbm, hidden_hbm, scale8_hbm, scale4_hbm, code8_hbm, code4_hbm,
     mixed_ref, token_ref, ratio_ref,
-    w8, w4, send1, gates1, recv1, grecv, send2, x_all, out8, back1, part, back2, sums, sums_all,
-    code_sem, s1, r1, sg, rg, s2, r2, sx, rx, se, re, sb, rb, sc, rc,
+    ids_ref, gate_ref, hidden_ref, scale8_ref, scale4_ref, w8, w4, send1, gates1, recv1, grecv, send2, x_all, out8, back1, part, back2, sums, sums_all,
+    small_sem, code_sem, s1, r1, sg, rg, s2, r2, sx, rx, se, re, sb, rb, sc, rc,
 ):
     zs, rs, xs, tok, top = sizes
     routes = tok * top
@@ -53,51 +53,79 @@
     me, tn = lax.axis_index("expert"), lax.axis_index("tensor")
     z, r = me // rs, lax.rem(me, rs)
 
+    def far_first(d, count):
+        step = d // 2
+        return count // 2 + jnp.where(d % 2 == 1, -step, step)
+
     def in_column(d):
-        return lax.rem(z + d, zs)
+        return lax.rem(z + far_first(d, zs), zs)
 
     def in_row(d):
-        return lax.rem(r + d, rs)
+        return lax.rem(r + far_first(d, rs), rs)
 
     def in_gather(d):
         return lax.rem(tn + d, xs)
 
+    small = (
+        (ids_hbm, ids_ref),
+        (gate_hbm, gate_ref),
+        (hidden_hbm, hidden_ref),
+        (scale8_hbm, scale8_ref),
+        (scale4_hbm, scale4_ref),
+    )
+    small_copies = []
+    for n, (src, dst) in enumerate(small):
+        copy = pltpu.make_async_copy(src, dst, small_sem.at[n])
+        copy.start()
+        small_copies.append(copy)
+
+    barrier = pltpu.get_barrier_semaphore()
+
+    @pl.loop(1, zs)
+    def _(d):
+        pl.semaphore_signal(
+            barrier, inc=1, device_id={"expert": in_column(d) * rs + r}, device_id_type=MESH
+        )
+
+    @pl.loop(1, rs)
+    def _(d):
+        pl.semaphore_signal(
+            barrier, inc=1, device_id={"expert": z * rs + in_row(d)}, device_id_type=MESH
+        )
+
+    @pl.loop(1, xs)
+    def _(d):
+        pl.semaphore_signal(barrier, inc=1, device_id={"tensor": in_gather(d)}, device_id_type=MESH)
+
     part_rows = inner // 2
     code_copies = []
-    for n, (src, dst) in enumerate(((code8_ref, w8), (code4_ref, w4))):
+    for n, (src, dst) in enumerate(((code8_hbm, w8), (code4_hbm, w4))):
         for h in range(2):
             piece = pl.ds(h * part_rows, part_rows)
             copy = pltpu.make_async_copy(src.at[0, piece, :], dst.at[piece, :], code_sem.at[n, h])
             copy.start()
             code_copies.append(copy)
 
-    barrier = pltpu.get_barrier_semaphore()
-
-    @pl.loop(1, zs)
-    def _(d):
-        pl.semaphore_signal(
-            barrier, inc=1, device_id={"expert": in_column(d) * rs + r}, device_id_type=MESH
-        )
-
-    @pl.loop(1, rs)
-    def _(d):
-        pl.semaphore_signal(
-            barrier, inc=1, device_id={"expert": z * rs + in_row(d)}, device_id_type=MESH
-        )
-
-    @pl.loop(1, xs)
-    def _(d):
-        pl.semaphore_signal(barrier, inc=1, device_id={"tensor": in_gather(d)}, device_id_type=MESH)
-
-    ids = jnp.broadcast_to(ids_ref[...], (routes, routes))
+    for copy in small_copies[:3]:
+        copy.wait()
+    gate = gate_ref[...]
+    high = gate.astype(bf16).astype(f32)
+    table = jnp.concatenate([ids_ref[...].astype(f32), high, gate - high], axis=0).astype(bf16)
+    repeat = (iota((tok, routes), 0) == iota((tok, routes), 1) // top).astype(f32).astype(bf16)
+    table = dot(table, repeat)
+    own_choice = iota((top, routes), 0) == iota((top, routes), 1) % top
+
+    def flat(n):
+        rows_of = table[n * top : (n + 1) * top]
+        return jnp.sum(jnp.where(own_choice, rows_of, 0.0), axis=0, keepdims=True)
+
+    flat_ids, gate_high, gate_low = flat(0), flat(1), flat(2)
+    ids = jnp.broadcast_to(flat_ids, (routes, routes))
     earlier = (ids == ids.T) & (iota((routes, routes), 0) < iota((routes, routes), 1))
-    position = jnp.sum(earlier.astype(jnp.int32), axis=0, keepdims=True)
-    target = ids_ref[...] * SLOTS + position
+    position = jnp.sum(jnp.where(earlier, 1.0, 0.0), axis=0, keepdims=True)
+    target = (flat_ids * SLOTS + position).astype(jnp.int32)
     chosen = iota((rows, routes), 0) == target
     select = chosen.astype(f32).astype(bf16)
-    gate = gate_ref[...]
-    gate_high = gate.astype(bf16).astype(f32)
-    gate_low = gate - gate_high
     lanes = gates1.shape[1]
     token_of = iota((routes, lanes), 0) // top
     place = iota((routes, lanes), 1)
@@ -155,11 +183,6 @@
         there = in_column(d)
         column_copy(send1.at[z_block(there)], recv1.at[z_block(z)], there, s1, r1).start()
 
-    @pl.loop(1, zs)
-    def _(d):
-        there = in_column(d)
-        column_copy(gates1.at[z_block(there)], grecv.at[z_block(z)], there, sg, rg).start()
-
     recv1[z_block(z), :] = send1[z_block(z), :]
     grecv[z_block(z), :] = gates1[z_block(z), :]
 
@@ -169,11 +192,11 @@
             group = pl.ds(pl.multiple_of(g * BLOCK, BLOCK), BLOCK)
             for b in range(feats // BLOCK):
                 cols = pl.ds(b * BLOCK, BLOCK)
-                w8[group, cols] = (w8[group, cols].astype(f32) * scale8_ref[0, g, b]).astype(bf16)
+                w8[group, cols] = (w8[group, cols].astype(f32) * scale8_ref[b, 0, g]).astype(bf16)
             w4[group, :] = (w4[group, :].astype(f32) * scale4_ref[0, pl.ds(g, 1), :]).astype(bf16)
 
     groups = inner // BLOCK
-    for copy in code_copies:
+    for copy in small_copies[3:] + code_copies:
         copy.wait()
     scale_weights(0, groups // 4)
 
@@ -193,7 +216,22 @@
         there = in_row(d)
         row_copy(send2.at[r_block(there)], x_all.at[r_block(r), mine], there, s2, r2).start()
 
+    @pl.loop(1, zs)
+    def _(d):
+        there = in_column(d)
+        column_copy(gates1.at[z_block(there)], grecv.at[z_block(z)], there, sg, rg).start()
+
     x_all[r_block(r), mine] = send2[r_block(r), :]
+
+    scale_weights(groups // 4, groups // 2)
+
+    all_but_r = pl.ds(0, rows - r_rows)
+    wait_2 = row_copy(send2.at[all_but_r], x_all.at[all_but_r, mine], r, s2, r2)
+    wait_2.wait_recv()
+
+    @pl.loop(1, xs)
+    def _(d):
+        gather_copy(x_all.at[:, mine], x_all.at[:, mine], in_gather(d), sx, rx).start()
 
     wait_g = column_copy(gates1.at[all_but_one], grecv.at[all_but_one], z, sg, rg)
     wait_g.wait_recv()
@@ -205,16 +243,6 @@
     row_z = iota((rows, 2 * tokens), 0) % r_rows // SLOTS
     lane_z = iota((rows, 2 * tokens), 1) % tokens // tok
     combine = jnp.where(row_z == lane_z, wide_gates, 0.0).T.astype(bf16)
-
-    scale_weights(groups // 4, groups // 2)
-
-    all_but_r = pl.ds(0, rows - r_rows)
-    wait_2 = row_copy(send2.at[all_but_r], x_all.at[all_but_r, mine], r, s2, r2)
-    wait_2.wait_recv()
-
-    @pl.loop(1, xs)
-    def _(d):
-        gather_copy(x_all.at[:, mine], x_all.at[:, mine], in_gather(d), sx, rx).start()
 
     scale_weights(groups // 2, groups)
     others = pl.ds(0, (xs - 1) * width)
@@ -353,7 +381,7 @@
     chunks = chunks_of(feats)
     count, tokens = len(chunks), zs * tok
     wide = max(chunks[-1][1] + BLOCK, chunks[0][1])
-    vmem, smem = pl.BlockSpec(memory_space=pltpu.VMEM), pl.BlockSpec(memory_space=pltpu.SMEM)
+    vmem = pl.BlockSpec(memory_space=pltpu.VMEM)
     dma = pltpu.SemaphoreType.DMA
     mixed, token, ratio = pl.pallas_call(
         functools.partial(kernel, sizes),
@@ -362,10 +390,14 @@
             jax.ShapeDtypeStruct((1, tok), f32),
             jax.ShapeDtypeStruct((1, 1), f32),
         ),
-        in_specs=[vmem, vmem, vmem, smem, vmem]
-        + [pl.BlockSpec(memory_space=pl.ANY)] * 2,
+        in_specs=[pl.BlockSpec(memory_space=pltpu.HBM)] * 7,
         out_specs=(vmem, vmem, vmem),
         scratch_shapes=[
+            pltpu.VMEM((top, tok), jnp.int32),
+            pltpu.VMEM((top, tok), f32),
+            pltpu.VMEM((routes, width), bf16),
+            pltpu.SMEM((feats // BLOCK, 1, inner // BLOCK), f32),
+            pltpu.VMEM((1, inner // BLOCK, feats), f32),
             pltpu.VMEM((inner, feats), bf16),
             pltpu.VMEM((inner, feats), bf16),
             pltpu.VMEM((rows, width), bf16),
@@ -380,21 +412,27 @@
             pltpu.VMEM((count, tokens, wide), bf16),
             pltpu.VMEM((8, rows), f32),
             pltpu.VMEM((xs, 8, rows), f32),
+            dma((5,)),
             dma((2, 2)),
         ]
         + [dma] * 10
         + [dma((count,))] * 4,
         compiler_params=pltpu.CompilerParams(
-            collective_id=0, has_side_effects=True, vmem_limit_bytes=32 * 1024 * 1024
+            collective_id=0, has_side_effects=True, vmem_limit_bytes=24 * 1024 * 1024
         ),
     )(
-        ids.reshape(1, routes),
-        gates.reshape(1, routes),
-        hidden.reshape(routes, width),
-        scale8,
-        scale4,
-        code8,
-        code4,
+        *[
+            pltpu.with_memory_space_constraint(operand, pltpu.HBM)
+            for operand in (
+                ids.T,
+                gates.T,
+                hidden.reshape(routes, width),
+                jnp.transpose(scale8, (2, 0, 1)),
+                scale4,
+                code8,
+                code4,
+            )
+        ]
     )
     return mixed, token.reshape(tok), ratio.reshape(1)
 

time: 68.6 us -> 57 us (0.83)
  local copies, waits for them, and re-layouts: 8.15 us -> 1.12 us
  Pallas kernels: 57.6 us -> 53.4 us
    unnamed x13 -> x2, local copies, waits for them, and re-layouts: 7.98 us -> 1.12 us
    pallas_call x1, Pallas kernels: 57.6 us -> 53.4 us  [per_device(): pl.pallas_call(functools.partial(kernel, sizes), out_shape=(jax.ShapeDtyp...]
where the time goes in v2:
time: 57 us; the launch traced here: 56.8 us
  Pallas kernels  53.4 us (94%)
  between operations  2.33 us (4%)
  local copies, waits for them, and re-layouts  1.12 us (2%)
    pallas_call x1, Pallas kernels, per_device(): pl.pallas_call(functools.partial(kernel, sizes), out_shape=(jax.ShapeDtyp...  53.4 us

profile of v2, /device:TPU:1, one launch (start us, length us, event | category | flops | bytes accessed | tf_op | source)
XLA Modules:
  0.0 56.8 jit_solution(17852430682413201863)
XLA Ops:
  0.6 53.4 %shard_map.94 = (bf16[16,896]{1,0:T(8,128)(2,1)S(1)}, f32[1,16]{1,0:T(1,128)S(1)}, f32[1,1]{1,0:T(1,128)}) custom-call(s32[8,16]{1,0:T(8,128)} %bitcast.8, f32[8,16]{1,0:T(8,128)} %bitcast.9, bf16[128,256]{1,0:T(8,128)(2,1)} %bitcast.7, f32[7,1,8]{2,1,0:T(1,128)} %bitcast.10, f32[1,8,896]{2,1,0:T(8,128)} %scale4_hbm.1, bf16[1,1024,896]{2,1,0:T(8,128)(2,1)} %code8_hbm.1, ...), custom_call_target="tpu_custom_call" | custom-call | tf_op jit(solution)/shard_map/pallas_call | solution.py:386
  54.0 0.6 %copy.13 = bf16[16,896]{1,0:T(8,128)(2,1)} copy(bf16[16,896]{1,0:T(8,128)(2,1)S(1)} %get-tuple-element.12) | data formatting | bytes 57344
  54.6 0.5 copy.14

commit v3 on v2

v3 whole, which is shorter than its diff:
```python
import functools

import jax
import jax.numpy as jnp
from jax import lax
from jax.experimental import pallas as pl
from jax.experimental.pallas import tpu as pltpu
from jax.sharding import PartitionSpec as P

BLOCK = 128
SLOTS = 2
SIDE = 8
CORES = 2
MESH = pl.DeviceIdType.MESH
f32, bf16 = jnp.float32, jnp.bfloat16


def iota(shape, dim):
    return lax.broadcasted_iota(jnp.int32, shape, dim)


def dot(a, b):
    return jnp.dot(a, b, preferred_element_type=f32)


def split3(value):
    high = value.astype(bf16).astype(f32)
    rest = value - high
    middle = rest.astype(bf16).astype(f32)
    return high, middle, rest - middle


def chunks_of(width):
    full = 2 * BLOCK
    pieces = [(s, min(full, width - s)) for s in range(0, width, full)]
    chunks = [(1 - n % 2, start, size) for n, (start, size) in enumerate(pieces)]
    return chunks + [(0, width, BLOCK)]


class Path:
    def __init__(self, number, me):
        rest = lax.rem(me, SIDE * CORES)
        z, y, core = me // (SIDE * CORES), rest // CORES, lax.rem(rest, CORES)
        self.number, self.core = number, core
        self.place, self.other = (z, y) if number == 0 else (y, z)
        self.spot = self.other * CORES + core

    def column(self, there):
        if self.number == 0:
            return there * (SIDE * CORES) + self.spot
        return self.other * (SIDE * CORES) + there * CORES + self.core

    def row(self, there):
        if self.number == 0:
            return self.place * (SIDE * CORES) + there
        return there // CORES * (SIDE * CORES) + self.place * CORES + lax.rem(there, CORES)


def far_first(d, count):
    step = d // 2
    return count // 2 + jnp.where(d % 2 == 1, -step, step)


def kernel(
    sizes,
    ids_hbm, gate_hbm, hidden_hbm, scale8_hbm, scale4_hbm, code8_hbm, code4_hbm,
    mixed_ref, token_ref, ratio_ref,
    ids_ref, gate_ref, hidden_ref, scale8_ref, scale4_ref, w8, w4, send1, gates1, recv1, grecv,
    send2, x_all, x_turned, sums, sums_all, outs, backs, parts, ends,
    small_sem, code_sem, s1, r1, sg, rg, s2, r2, sx, rx, se, re, sb, rb, sc, rc,
):
    xs, tok, top = sizes
    routes = tok * top
    spots = SIDE * CORES
    rows = SIDE * spots * SLOTS
    c_rows, r_rows = spots * SLOTS, SIDE * SLOTS
    tokens = SIDE * tok
    width = hidden_ref.shape[1]
    inner, feats = w8.shape
    chunks = chunks_of(feats)
    last = len(chunks) - 1

    me, tn = lax.axis_index("expert"), lax.axis_index("tensor")
    paths = Path(0, me), Path(1, me)
    first = paths[0]

    def in_column(path, d):
        return lax.rem(path.place + far_first(d, SIDE), SIDE)

    def in_row(path, d):
        return lax.rem(path.spot + far_first(d, spots), spots)

    def in_gather(d):
        return lax.rem(tn + d, xs)

    small = (
        (ids_hbm, ids_ref),
        (gate_hbm, gate_ref),
        (hidden_hbm, hidden_ref),
        (scale8_hbm, scale8_ref),
        (scale4_hbm, scale4_ref),
    )
    small_copies = []
    for n, (src, dst) in enumerate(small):
        copy = pltpu.make_async_copy(src, dst, small_sem.at[n])
        copy.start()
        small_copies.append(copy)

    barrier = pltpu.get_barrier_semaphore()

    def signal(device):
        pl.semaphore_signal(barrier, inc=1, device_id=device, device_id_type=MESH)

    @pl.loop(1, SIDE)
    def _(d):
        for path in paths:
            step = in_column(path, d) * CORES
            for core in range(CORES):
                signal({"expert": paths[1 - path.number].row(step + core)})

    signal({"expert": first.row(first.other * CORES + 1 - first.core)})

    @pl.loop(1, xs)
    def _(d):
        signal({"tensor": in_gather(d)})

    part_rows = inner // 2
    code_copies = []
    for n, (src, dst) in enumerate(((code8_hbm, w8), (code4_hbm, w4))):
        for h in range(2):
            piece = pl.ds(h * part_rows, part_rows)
            copy = pltpu.make_async_copy(src.at[0, piece, :], dst.at[piece, :], code_sem.at[n, h])
            copy.start()
            code_copies.append(copy)

    for copy in small_copies[:3]:
        copy.wait()
    gate = gate_ref[...]
    high = gate.astype(bf16).astype(f32)
    table = jnp.concatenate([ids_ref[...].astype(f32), high, gate - high], axis=0).astype(bf16)
    repeat = (iota((tok, routes), 0) == iota((tok, routes), 1) // top).astype(f32).astype(bf16)
    table = dot(table, repeat)
    own_choice = iota((top, routes), 0) == iota((top, routes), 1) % top

    def flat(n):
        rows_of = table[n * top : (n + 1) * top]
        return jnp.sum(jnp.where(own_choice, rows_of, 0.0), axis=0, keepdims=True)

    flat_ids, gate_high, gate_low = flat(0), flat(1), flat(2)
    ids = jnp.broadcast_to(flat_ids, (routes, routes))
    earlier = (ids == ids.T) & (iota((routes, routes), 0) < iota((routes, routes), 1))
    position = jnp.sum(jnp.where(earlier, 1.0, 0.0), axis=0, keepdims=True).astype(jnp.int32)
    expert = flat_ids.astype(jnp.int32)
    target = expert % spots * r_rows + expert // spots * SLOTS + position
    chosen = iota((rows, routes), 0) == target
    send1[...] = dot(chosen.astype(f32).astype(bf16), hidden_ref[...]).astype(bf16)

    pl.semaphore_wait(barrier, 2 * (SIDE - 1) + spots - 1 + xs - 1)

    def copy_to(device, src, dst, send, recv):
        return pltpu.make_async_remote_copy(
            src_ref=src,
            dst_ref=dst,
            send_sem=send,
            recv_sem=recv,
            device_id=device,
            device_id_type=MESH,
        )

    here = {"expert": me}

    def c_block(n):
        return pl.ds(pl.multiple_of(n * c_rows, c_rows), c_rows)

    def r_block(n):
        return pl.ds(pl.multiple_of(n * r_rows, r_rows), r_rows)

    def t_block(n):
        return pl.ds(pl.multiple_of(n * tok, tok), tok)

    def row_exchange(path, src, dst, send, recv):
        @pl.loop(1, spots)
        def _(d):
            there = in_row(path, d)
            copy_to(
                {"expert": path.row(there)},
                src.at[r_block(there)],
                dst.at[r_block(path.spot)],
                send,
                recv,
            ).start()

    def column_exchange(path, src, dst, send, recv):
        @pl.loop(1, SIDE)
        def _(d):
            there = in_column(path, d)
            copy_to(
                {"expert": path.column(there)},
                src.at[c_block(there)],
                dst.at[c_block(path.place)],
                send,
                recv,
            ).start()

    row_exchange(first, send1, recv1, s1, r1)
    recv1[r_block(first.spot), :] = send1[r_block(first.spot), :]

    lanes = gates1.shape[2]
    token_of = iota((routes, lanes), 0) // top
    lane = iota((routes, lanes), 1)
    spread_high = (lane == token_of).astype(f32).astype(bf16)
    spread_low = (lane == token_of + tok).astype(f32).astype(bf16)
    turned = expert // CORES % SIDE * c_rows + expert // spots * CORES * SLOTS
    turned = turned + expert % CORES * SLOTS + position
    for path, target in zip(paths, (expert * SLOTS + position, turned)):
        chosen = iota((rows, routes), 0) == target
        gates = dot(jnp.where(chosen, gate_high, 0.0).astype(bf16), spread_high)
        gates = gates + dot(jnp.where(chosen, gate_low, 0.0).astype(bf16), spread_low)
        gates1[path.number] = gates.astype(bf16)

    def scale_weights(begin, end):
        @pl.loop(begin, end)
        def _(g):
            group = pl.ds(pl.multiple_of(g * BLOCK, BLOCK), BLOCK)
            for b in range(feats // BLOCK):
                cols = pl.ds(b * BLOCK, BLOCK)
                w8[group, cols] = (w8[group, cols].astype(f32) * scale8_ref[b, 0, g]).astype(bf16)
            w4[group, :] = (w4[group, :].astype(f32) * scale4_ref[0, pl.ds(g, 1), :]).astype(bf16)

    groups = inner // BLOCK
    for copy in small_copies[3:] + code_copies:
        copy.wait()
    scale_weights(0, groups // 4)

    at, of = iota((rows, rows), 0), iota((rows, rows), 1)
    low_place, slot = at % r_rows // SLOTS, at % SLOTS
    reorder = of == low_place * c_rows + at // r_rows * SLOTS + slot
    reorder = reorder.astype(f32).astype(bf16)
    turn = of == low_place * c_rows + at % c_rows // r_rows * r_rows + at // c_rows * SLOTS + slot
    turn = turn.astype(f32).astype(bf16)

    but_c, but_r = pl.ds(0, rows - c_rows), pl.ds(0, rows - r_rows)
    wait_1 = copy_to(here, send1.at[but_r], recv1.at[but_r], s1, r1)
    wait_1.wait_recv()
    send2[...] = dot(turn, recv1[...]).astype(bf16)

    mine = pl.ds(pl.multiple_of(tn * width, width), width)
    arrived = x_all.at[:, mine]
    column_exchange(first, send2, arrived, s2, r2.at[first.place])
    x_all[c_block(first.place), mine] = send2[c_block(first.place), :]
    for path in paths:
        n = path.number
        column_exchange(path, gates1.at[n], grecv.at[n], sg.at[n], rg.at[n])
        grecv[n, c_block(path.place), :] = gates1[n, c_block(path.place), :]

    scale_weights(groups // 4, groups // 2)

    for n in range(SIDE):
        step = n // 2 if n % 2 == 0 else -(n // 2 + 1)
        source = lax.rem(first.place + SIDE + step, SIDE)
        block = c_block(source)
        if n > 0:
            copy_to(here, send2.at[block], arrived.at[block], s2, r2.at[source]).wait_recv()

        @pl.loop(1, xs)
        def _(d):
            copy_to(
                {"tensor": in_gather(d)}, arrived.at[block], arrived.at[block], sx, rx
            ).start()

    wait_2 = copy_to(here, send2.at[but_c], arrived.at[but_c], s2, r2.at[0])

    place, wide = iota((lanes, 2 * tokens), 0), iota((lanes, 2 * tokens), 1)
    widen = (place == wide % tok + jnp.where(wide < tokens, 0, tok)).astype(f32).astype(bf16)
    row_place = iota((rows, 2 * tokens), 0) % r_rows // SLOTS
    own_place = row_place == iota((rows, 2 * tokens), 1) % tokens // tok
    combine, waits_g = [], []
    for path in paths:
        n = path.number
        wait_g = copy_to(here, gates1.at[n, but_c], grecv.at[n, but_c], sg.at[n], rg.at[n])
        wait_g.wait_recv()
        waits_g.append(wait_g)
        gates = dot(dot(reorder, grecv[n]).astype(bf16), widen)
        combine.append(jnp.where(own_place, gates, 0.0).T.astype(bf16))

    scale_weights(groups // 2, groups)
    others = pl.ds(0, (xs - 1) * width)
    wait_x = copy_to(here, x_all.at[:, others], x_all.at[:, others], sx, rx)
    wait_x.wait_recv()

    def send_back(c):
        path = paths[chunks[c][0]]

        @pl.loop(1, spots)
        def _(d):
            there = in_row(path, d)
            copy_to(
                {"expert": path.row(there)},
                outs[c].at[r_block(there)],
                backs[c].at[r_block(path.spot)],
                sb.at[c],
                rb.at[c],
            ).start()

        backs[c][r_block(path.spot), :] = outs[c][r_block(path.spot), :]

    early = min(2, last)
    for c, (number, start, size) in enumerate(chunks[:last]):
        if c == 1:
            x_turned[...] = dot(turn, x_all[...]).astype(bf16)
        activation = x_all if number else x_turned
        outs[c][...] = dot(activation[...], w8[:, start : start + size]).astype(bf16)
        if c < early:
            send_back(c)
    gap_sums = [jnp.zeros((rows, BLOCK), f32), jnp.zeros((rows, BLOCK), f32)]
    ref_sum = jnp.zeros((rows, BLOCK), f32)
    for c, (number, start, size) in enumerate(chunks[:last]):
        activation = x_all if number else x_turned
        result4 = dot(activation[...], w4[:, start : start + size]).astype(bf16).astype(f32)
        result8 = outs[c][...].astype(f32)
        gap = result4 - result8
        for b in range(size // BLOCK):
            cols = slice(b * BLOCK, (b + 1) * BLOCK)
            gap_sums[number] += gap[:, cols] * gap[:, cols]
            ref_sum += result8[:, cols] * result8[:, cols]

    def stack3(value, count):
        high, middle, low = split3(value)
        which = iota((count, rows), 0)
        low = jnp.where(which == 2, low, 0.0)
        return jnp.where(which == 0, high, jnp.where(which == 1, middle, low)).astype(bf16)

    gap_rows = [jnp.sum(gap_sum.T, axis=0, keepdims=True) for gap_sum in gap_sums]
    moved = jnp.sum(dot(stack3(gap_rows[1], 8), turn), axis=0, keepdims=True)
    gap_row = gap_rows[0] + moved
    outs[last][...] = stack3(gap_row, BLOCK).astype(f32).T.astype(bf16)
    for c in [last] + list(range(early, last)):
        send_back(c)
    gap_part = jnp.sum(gap_row, axis=1, keepdims=True)
    ref_part = jnp.sum(jnp.sum(ref_sum, axis=0, keepdims=True), axis=1, keepdims=True)

    def wait_back(c):
        return copy_to(here, outs[c].at[but_r], backs[c].at[but_r], sb.at[c], rb.at[c])

    def wait_end(c):
        some = pl.ds(0, SIDE - 1) if c == last else pl.ds(0, tokens - tok)
        return copy_to(here, ends[c].at[some], ends[c].at[some], sc.at[c], rc.at[c])

    def combine_and_send(c):
        path = paths[chunks[c][0]]
        wait_back(c).wait_recv()
        both = dot(combine[path.number], backs[c][...])
        total = both[:tokens] + both[tokens:]
        if c == last:
            error = jnp.sum(total, axis=1, keepdims=True)
            parts[c][...] = jnp.broadcast_to(error, (tokens, BLOCK)).T[:8]
        else:
            parts[c][...] = total.astype(bf16)

        @pl.loop(1, SIDE)
        def _(d):
            there = in_column(path, d)
            copy_to(
                {"expert": path.column(there)},
                parts[c] if c == last else parts[c].at[t_block(there)],
                ends[c].at[path.place] if c == last else ends[c].at[t_block(path.place)],
                sc.at[c],
                rc.at[c],
            ).start()

        if c == last:
            ends[c][path.place] = parts[c][...]
        else:
            ends[c][t_block(path.place), :] = parts[c][t_block(path.place), :]

    order = list(range(early)) + [last] + list(range(early, last))
    for c in order:
        combine_and_send(c)

    for c in order:
        wait_end(c).wait_recv()
        if c < last:
            _, start, size = chunks[c]
            total = ends[c][:tok].astype(f32)
            for n in range(1, SIDE):
                total = total + ends[c][n * tok : (n + 1) * tok].astype(f32)
            mixed_ref[:, start : start + size] = total.astype(bf16)
        else:
            total = ends[c][0]
            for n in range(1, SIDE):
                total = total + ends[c][n]
            which = iota((8, tokens), 0)
            sums[...] = jnp.where(which == 0, total, jnp.where(which == 1, gap_part, ref_part))
            sums_all[tn] = sums[...]

            @pl.loop(1, xs)
            def _(d):
                copy_to({"tensor": in_gather(d)}, sums, sums_all.at[tn], se, re).start()

    sums_but = pl.ds(0, xs - 1)
    wait_e = copy_to(here, sums_all.at[sums_but], sums_all.at[sums_but], se, re)
    wait_e.wait_recv()
    total = sums_all[0]
    for n in range(1, xs):
        total = total + sums_all[n]
    ratio_ref[...] = total[1:2, :1] / (total[2:3, :1] + 1e-06)
    place = iota((tok, tokens), 1) - paths[chunks[last][0]].place * tok
    error = jnp.where(place == iota((tok, tokens), 0), total[0:1], 0.0)
    error = jnp.sum(error, axis=1, keepdims=True)
    diagonal = iota((tok, tok), 0) == iota((tok, tok), 1)
    token_ref[...] = jnp.sum(jnp.where(diagonal, error, 0.0), axis=0, keepdims=True)

    for wait in [wait_1, wait_2, wait_x, wait_e] + waits_g:
        wait.wait_send()
    for c in range(last + 1):
        wait_back(c).wait_send()
        wait_end(c).wait_send()


def per_device(sizes, hidden, ids, gates, code8, scale8, code4, scale4):
    xs, tok, top = sizes
    routes, width = tok * top, hidden.shape[2]
    rows = SIDE * SIDE * CORES * SLOTS
    inner, feats = code8.shape[1:]
    chunks = chunks_of(feats)
    count, tokens = len(chunks), SIDE * tok
    vmem = pl.BlockSpec(memory_space=pltpu.VMEM)
    dma = pltpu.SemaphoreType.DMA
    mixed, token, ratio = pl.pallas_call(
        functools.partial(kernel, sizes),
        out_shape=(
            jax.ShapeDtypeStruct((tok, feats), bf16),
            jax.ShapeDtypeStruct((1, tok), f32),
            jax.ShapeDtypeStruct((1, 1), f32),
        ),
        in_specs=[pl.BlockSpec(memory_space=pltpu.HBM)] * 7,
        out_specs=(vmem, vmem, vmem),
        scratch_shapes=[
            pltpu.VMEM((top, tok), jnp.int32),
            pltpu.VMEM((top, tok), f32),
            pltpu.VMEM((routes, width), bf16),
            pltpu.SMEM((feats // BLOCK, 1, inner // BLOCK), f32),
            pltpu.VMEM((1, inner // BLOCK, feats), f32),
            pltpu.VMEM((inner, feats), bf16),
            pltpu.VMEM((inner, feats), bf16),
            pltpu.VMEM((rows, width), bf16),
            pltpu.VMEM((2, rows, BLOCK), bf16),
            pltpu.VMEM((rows, width), bf16),
            pltpu.VMEM((2, rows, BLOCK), bf16),
            pltpu.VMEM((rows, width), bf16),
            pltpu.VMEM((rows, xs * width), bf16),
            pltpu.VMEM((rows, xs * width), bf16),
            pltpu.VMEM((8, tokens), f32),
            pltpu.VMEM((xs, 8, tokens), f32),
            [pltpu.VMEM((rows, size), bf16) for _, _, size in chunks],
            [pltpu.VMEM((rows, size), bf16) for _, _, size in chunks],
            [pltpu.VMEM((tokens, size), bf16) for _, _, size in chunks[:-1]]
            + [pltpu.VMEM((8, tokens), f32)],
            [pltpu.VMEM((tokens, size), bf16) for _, _, size in chunks[:-1]]
            + [pltpu.VMEM((SIDE, 8, tokens), f32)],
            dma((5,)),
            dma((2, 2)),
            dma,
            dma,
            dma((2,)),
            dma((2,)),
            dma,
            dma((SIDE,)),
        ]
        + [dma] * 4
        + [dma((count,))] * 4,
        compiler_params=pltpu.CompilerParams(
            collective_id=0, has_side_effects=True, vmem_limit_bytes=24 * 1024 * 1024
        ),
    )(
        *[
            pltpu.with_memory_space_constraint(operand, pltpu.HBM)
            for operand in (
                ids.T,
                gates.T,
                hidden.reshape(routes, width),
                jnp.transpose(scale8, (2, 0, 1)),
                scale4,
                code8,
                code4,
            )
        ]
    )
    return mixed, token.reshape(tok), ratio.reshape(1)


def solution(mesh):
    experts, xs = mesh.shape["expert"], mesh.shape["tensor"]
    assert experts == SIDE * SIDE * CORES

    def run(hidden, *rest):
        tok, top = hidden.shape[0] // experts, hidden.shape[1]
        mapped = jax.shard_map(
            functools.partial(per_device, (xs, tok, top)),
            mesh=mesh,
            in_specs=(
                P("expert", None, "tensor"),
                P("expert", None),
                P("expert", None),
                P("expert", None, "tensor"),
                P("expert", None, "tensor"),
                P("expert", None, "tensor"),
                P("expert", None, "tensor"),
            ),
            out_specs=(P("expert", "tensor"), P("expert"), P("expert")),
            check_vma=False,
        )
        return mapped(hidden, *rest)

    return run
```

time: 57 us -> 53.5 us (0.939)
  Pallas kernels: 53.4 us -> 49.5 us
    pallas_call x1, Pallas kernels: 53.4 us -> 49.5 us  [per_device(): pl.pallas_call(functools.partial(kernel, sizes), out_shape=(jax.ShapeDtyp...]
where the time goes in v3:
time: 53.5 us; the launch traced here: 53 us
  Pallas kernels  49.5 us (93%)
  between operations  2.33 us (4%)
  local copies, waits for them, and re-layouts  1.12 us (2%)
    pallas_call x1, Pallas kernels, per_device(): pl.pallas_call(functools.partial(kernel, sizes), out_shape=(jax.ShapeDtyp...  49.5 us
    unnamed x2, local copies, waits for them, and re-layouts  1.12 us

profile of v3, /device:TPU:1, one launch (start us, length us, event | category | flops | bytes accessed | tf_op | source)
XLA Modules:
  0.0 53.0 jit_solution(15430278364171178019)
XLA Ops:
  0.6 49.5 %shard_map.94 = (bf16[16,896]{1,0:T(8,128)(2,1)S(1)}, f32[1,16]{1,0:T(1,128)S(1)}, f32[1,1]{1,0:T(1,128)}) custom-call(s32[8,16]{1,0:T(8,128)} %bitcast.8, f32[8,16]{1,0:T(8,128)} %bitcast.9, bf16[128,256]{1,0:T(8,128)(2,1)} %bitcast.7, f32[7,1,8]{2,1,0:T(1,128)} %bitcast.10, f32[1,8,896]{2,1,0:T(8,128)} %scale4_hbm.1, bf16[1,1024,896]{2,1,0:T(8,128)(2,1)} %code8_hbm.1, ...), custom_call_target="tpu_custom_call" | custom-call | tf_op jit(solution)/shard_map/pallas_call | solution.py:429
  50.2 0.6 %copy.13 = bf16[16,896]{1,0:T(8,128)(2,1)} copy(bf16[16,896]{1,0:T(8,128)(2,1)S(1)} %get-tuple-element.12) | data formatting | bytes 57344
  50.8 0.5 copy.14

commit v4 on v3

--- a/solution.py
+++ b/solution.py
@@ -11,6 +11,7 @@
 SLOTS = 2
 SIDE = 8
 CORES = 2
+EARLY = 2
 MESH = pl.DeviceIdType.MESH
 f32, bf16 = jnp.float32, jnp.bfloat16
 
@@ -32,9 +33,10 @@
 
 def chunks_of(width):
     full = 2 * BLOCK
-    pieces = [(s, min(full, width - s)) for s in range(0, width, full)]
-    chunks = [(1 - n % 2, start, size) for n, (start, size) in enumerate(pieces)]
-    return chunks + [(0, width, BLOCK)]
+    starts = [0] + list(range(width % full or full, width, full))
+    ends = starts[1:] + [width]
+    chunks = [(1 - n % 2, a, b - a) for n, (a, b) in enumerate(zip(starts, ends))]
+    return chunks + [(1, width, BLOCK)]
 
 
 class Path:
@@ -93,6 +95,24 @@
     def in_gather(d):
         return lax.rem(tn + d, xs)
 
+    barrier = pltpu.get_barrier_semaphore()
+
+    def signal(device):
+        pl.semaphore_signal(barrier, inc=1, device_id=device, device_id_type=MESH)
+
+    @pl.loop(1, SIDE)
+    def _(d):
+        for path in paths:
+            step = in_column(path, d) * CORES
+            for core in range(CORES):
+                signal({"expert": paths[1 - path.number].row(step + core)})
+
+    signal({"expert": first.row(first.other * CORES + 1 - first.core)})
+
+    @pl.loop(1, xs)
+    def _(d):
+        signal({"tensor": in_gather(d)})
+
     small = (
         (ids_hbm, ids_ref),
         (gate_hbm, gate_ref),
@@ -105,25 +125,6 @@
         copy = pltpu.make_async_copy(src, dst, small_sem.at[n])
         copy.start()
         small_copies.append(copy)
-
-    barrier = pltpu.get_barrier_semaphore()
-
-    def signal(device):
-        pl.semaphore_signal(barrier, inc=1, device_id=device, device_id_type=MESH)
-
-    @pl.loop(1, SIDE)
-    def _(d):
-        for path in paths:
-            step = in_column(path, d) * CORES
-            for core in range(CORES):
-                signal({"expert": paths[1 - path.number].row(step + core)})
-
-    signal({"expert": first.row(first.other * CORES + 1 - first.core)})
-
-    @pl.loop(1, xs)
-    def _(d):
-        signal({"tensor": in_gather(d)})
-
     part_rows = inner // 2
     code_copies = []
     for n, (src, dst) in enumerate(((code8_hbm, w8), (code4_hbm, w4))):
@@ -304,7 +305,7 @@
 
         backs[c][r_block(path.spot), :] = outs[c][r_block(path.spot), :]
 
-    early = min(2, last)
+    early = min(EARLY, last)
     for c, (number, start, size) in enumerate(chunks[:last]):
         if c == 1:
             x_turned[...] = dot(turn, x_all[...]).astype(bf16)
@@ -331,8 +332,9 @@
         return jnp.where(which == 0, high, jnp.where(which == 1, middle, low)).astype(bf16)
 
     gap_rows = [jnp.sum(gap_sum.T, axis=0, keepdims=True) for gap_sum in gap_sums]
-    moved = jnp.sum(dot(stack3(gap_rows[1], 8), turn), axis=0, keepdims=True)
-    gap_row = gap_rows[0] + moved
+    last_path = chunks[last][0]
+    moved = jnp.sum(dot(stack3(gap_rows[1 - last_path], 8), turn), axis=0, keepdims=True)
+    gap_row = gap_rows[last_path] + moved
     outs[last][...] = stack3(gap_row, BLOCK).astype(f32).T.astype(bf16)
     for c in [last] + list(range(early, last)):
         send_back(c)

time: 53.5 us -> 52.8 us (0.987)
  no operation moved by 1% of the time
where the time goes in v4:
time: 52.8 us; the launch traced here: 52.7 us
  Pallas kernels  49.2 us (93%)
  between operations  2.33 us (4%)
  local copies, waits for them, and re-layouts  1.12 us (2%)
    pallas_call x1, Pallas kernels, per_device(): pl.pallas_call(functools.partial(kernel, sizes), out_shape=(jax.ShapeDtyp...  49.2 us
    unnamed x2, local copies, waits for them, and re-layouts  1.12 us

profile of v4, /device:TPU:1, one launch (start us, length us, event | category | flops | bytes accessed | tf_op | source)
XLA Modules:
  0.0 52.7 jit_solution(14463259249653675881)
XLA Ops:
  0.6 49.2 %shard_map.94 = (bf16[16,896]{1,0:T(8,128)(2,1)S(1)}, f32[1,16]{1,0:T(1,128)S(1)}, f32[1,1]{1,0:T(1,128)}) custom-call(s32[8,16]{1,0:T(8,128)} %bitcast.8, f32[8,16]{1,0:T(8,128)} %bitcast.9, bf16[128,256]{1,0:T(8,128)(2,1)} %bitcast.7, f32[7,1,8]{2,1,0:T(1,128)} %bitcast.10, f32[1,8,896]{2,1,0:T(8,128)} %scale4_hbm.1, bf16[1,1024,896]{2,1,0:T(8,128)(2,1)} %code8_hbm.1, ...), custom_call_target="tpu_custom_call" | custom-call | tf_op jit(solution)/shard_map/pallas_call | solution.py:431
  49.9 0.6 %copy.13 = bf16[16,896]{1,0:T(8,128)(2,1)} copy(bf16[16,896]{1,0:T(8,128)(2,1)S(1)} %get-tuple-element.12) | data formatting | bytes 57344
  50.5 0.5 copy.14

commit v5 on v4

--- a/solution.py
+++ b/solution.py
@@ -231,7 +231,7 @@
     groups = inner // BLOCK
     for copy in small_copies[3:] + code_copies:
         copy.wait()
-    scale_weights(0, groups // 4)
+    scale_weights(0, groups)
 
     at, of = iota((rows, rows), 0), iota((rows, rows), 1)
     low_place, slot = at % r_rows // SLOTS, at % SLOTS
@@ -253,8 +253,6 @@
         n = path.number
         column_exchange(path, gates1.at[n], grecv.at[n], sg.at[n], rg.at[n])
         grecv[n, c_block(path.place), :] = gates1[n, c_block(path.place), :]
-
-    scale_weights(groups // 4, groups // 2)
 
     for n in range(SIDE):
         step = n // 2 if n % 2 == 0 else -(n // 2 + 1)
@@ -284,7 +282,6 @@
         gates = dot(dot(reorder, grecv[n]).astype(bf16), widen)
         combine.append(jnp.where(own_place, gates, 0.0).T.astype(bf16))
 
-    scale_weights(groups // 2, groups)
     others = pl.ds(0, (xs - 1) * width)
     wait_x = copy_to(here, x_all.at[:, others], x_all.at[:, others], sx, rx)
     wait_x.wait_recv()

time: 52.8 us -> 52.8 us (level)
  no operation moved by 1% of the time
where the time goes in v5:
time: 52.8 us; the launch traced here: 52.7 us
  Pallas kernels  49.2 us (93%)
  between operations  2.33 us (4%)
  local copies, waits for them, and re-layouts  1.12 us (2%)
    pallas_call x1, Pallas kernels, per_device(): pl.pallas_call(functools.partial(kernel, sizes), out_shape=(jax.ShapeDtyp...  49.2 us
    unnamed x2, local copies, waits for them, and re-layouts  1.12 us

profile of v5, /device:TPU:1, one launch (start us, length us, event | category | flops | bytes accessed | tf_op | source)
XLA Modules:
  0.0 52.7 jit_solution(5161637306148586436)
XLA Ops:
  0.6 49.2 %shard_map.94 = (bf16[16,896]{1,0:T(8,128)(2,1)S(1)}, f32[1,16]{1,0:T(1,128)S(1)}, f32[1,1]{1,0:T(1,128)}) custom-call(s32[8,16]{1,0:T(8,128)} %bitcast.8, f32[8,16]{1,0:T(8,128)} %bitcast.9, bf16[128,256]{1,0:T(8,128)(2,1)} %bitcast.7, f32[7,1,8]{2,1,0:T(1,128)} %bitcast.10, f32[1,8,896]{2,1,0:T(8,128)} %scale4_hbm.1, bf16[1,1024,896]{2,1,0:T(8,128)(2,1)} %code8_hbm.1, ...), custom_call_target="tpu_custom_call" | custom-call | tf_op jit(solution)/shard_map/pallas_call | solution.py:428
  49.9 0.6 %copy.13 = bf16[16,896]{1,0:T(8,128)(2,1)} copy(bf16[16,896]{1,0:T(8,128)(2,1)S(1)} %get-tuple-element.12) | data formatting | bytes 57344
  50.5 0.5 copy.14
